TPU v7x, 256 devices: a whole 4x4x8 slice. The times are simulated.
256 devices in a mesh: expert: 16 (over z, core), dp: 4 (over x), tensor: 4 (over y).
Axes of the slice: x: 4, y: 4, z: 8, core: 2. Of those that a mesh axis runs over, the one named last changes fastest.
Arguments:
- grad_out: bfloat16 [8192, 2048], P('expert', ('dp', 'tensor')), may hold values from -9 to 9
- gate_prob: float32 [8192], P('expert'), may hold values from 0.1 to 1
- expert_ids: int32 [8192], P('expert'), may hold values from 0 to 15, as said below
- slot_index: int32 [8192], P('expert'), may hold values from -1 to 39, as said below
- saved_rows: bfloat16 [16, 1280, 2048], P('expert', 'dp'), may hold values from -6 to 6
- row_rank: int32 [16, 16, 40], P('expert'), may hold values from -1 to 639, as said below
- part_counts: int32 [16, 4], P('expert'), may hold values from 0 to 320, as said below
- w_gate: bfloat16 [16, 2048, 4096], P('expert', None, ('dp', 'tensor')), may hold values from -0.125 to 0.125
- w_up: bfloat16 [16, 2048, 4096], P('expert', None, ('dp', 'tensor')), may hold values from -0.125 to 0.125
- w_down: bfloat16 [16, 4096, 2048], P('expert', ('dp', 'tensor')), may hold values from -0.09375 to 0.09375
Outputs:
- grad_input: bfloat16 [8192, 2048], P('expert', ('dp', 'tensor'))
- grad_gate: bfloat16 [16, 2048, 4096], P('expert', None, ('dp', 'tensor'))
- grad_up: bfloat16 [16, 2048, 4096], P('expert', None, ('dp', 'tensor'))
- grad_down: bfloat16 [16, 4096, 2048], P('expert', ('dp', 'tensor'))
Inputs may be any that keep to these rules, and one draw needn't show every extreme that they name: `expert_ids`: in every draw one expert is chosen by 40 or more tokens of every group. `slot_index`: the number of earlier tokens of the same group with the same expert, or -1 once that number reaches 40. `row_rank`: -1 exactly where the slot holds no token (slot c of group s for expert e holds one when c < the number of tokens of group s with slot_index >= 0 and expert e); the slots of expert e that hold tokens take positions 0 to their number - 1, each once. part_counts[e] sums to the number of slots of expert e that hold tokens; expert e's compacted list lies in partition order, partition p holding its part_counts[e, p] positions in its first rows; in every draw some partition is full.
All inputs are finite; a program needn't handle non-finite values.
Results may differ from a plain program's by a relative error of at most 0.0057.
Values may be sent and summed in bfloat16 or wider, within the bound.
A program may use at most 64 MiB of HBM per device.

v0:
```python
import jax
import jax.numpy as jnp
from jax import lax
from jax.sharding import PartitionSpec as P


def locate(positions, counts, keep_cap):
    bounds = jnp.cumsum(counts)
    partition = jnp.sum((positions[..., None] >= bounds).astype(jnp.int32), axis=-1)
    below_part = jnp.arange(counts.shape[0], dtype=jnp.int32) < partition[..., None]
    offsets = jnp.sum(jnp.where(below_part, counts, 0), axis=-1)
    slot_kept = positions >= 0
    row_index = jnp.where(slot_kept, partition * keep_cap + positions - offsets, 0)
    return (slot_kept, row_index)


def expert_grads(inputs, grad_rows, gate_weight, up_weight, down_weight):
    gate_pre = jnp.dot(inputs, gate_weight, preferred_element_type=jnp.float32)
    up_pre = jnp.dot(inputs, up_weight, preferred_element_type=jnp.float32)
    squash = jax.nn.sigmoid(gate_pre)
    activated = gate_pre * squash
    hidden = (activated * up_pre).astype(jnp.bfloat16)
    hidden_grad = lax.dot_general(
        grad_rows, down_weight, (((1,), (1,)), ((), ())), preferred_element_type=jnp.float32
    )
    up_grad = (hidden_grad * activated).astype(jnp.bfloat16)
    gate_grad = (hidden_grad * up_pre * squash * (1.0 + gate_pre * (1.0 - squash))).astype(
        jnp.bfloat16
    )
    partial_value = lax.dot_general(
        gate_grad, gate_weight, (((1,), (1,)), ((), ())), preferred_element_type=jnp.float32
    )
    partial_value = partial_value + lax.dot_general(
        up_grad, up_weight, (((1,), (1,)), ((), ())), preferred_element_type=jnp.float32
    )
    gate_wgrad = lax.dot_general(
        inputs, gate_grad, (((0,), (0,)), ((), ())), preferred_element_type=jnp.float32
    )
    up_wgrad = lax.dot_general(
        inputs, up_grad, (((0,), (0,)), ((), ())), preferred_element_type=jnp.float32
    )
    down_wgrad = lax.dot_general(
        hidden, grad_rows, (((0,), (0,)), ((), ())), preferred_element_type=jnp.float32
    )
    return (
        partial_value,
        gate_wgrad.astype(jnp.bfloat16),
        up_wgrad.astype(jnp.bfloat16),
        down_wgrad.astype(jnp.bfloat16),
    )


def local(
    grad_out,
    gate_prob,
    expert_ids,
    slot_index,
    saved_rows,
    row_rank,
    part_counts,
    w_gate,
    w_up,
    w_down,
):
    experts = row_rank.shape[1]
    capacity = row_rank.shape[2]
    keep_cap = saved_rows.shape[1]
    target = jnp.where(slot_index >= 0, expert_ids * capacity + slot_index, experts * capacity)
    full_rows = lax.all_gather(grad_out, ("dp", "tensor"), axis=1, tiled=True)
    scaled = (gate_prob[:, None] * full_rows.astype(jnp.float32)).astype(jnp.bfloat16)
    features = scaled.shape[1]
    padded_table = (
        jnp.zeros((experts * capacity + 1, features), scaled.dtype).at[target].set(scaled)
    )
    grad_bins = lax.all_to_all(
        padded_table[:-1].reshape(experts, capacity, features),
        "expert",
        split_axis=0,
        concat_axis=0,
        tiled=True,
    )
    stored = lax.all_gather(saved_rows, "dp", axis=1, tiled=True)[0]
    slot_kept, row_index = locate(row_rank[0], part_counts[0], keep_cap)
    picked = jnp.take(stored, row_index.reshape(-1), axis=0)
    inputs = jnp.where(slot_kept.reshape(-1, 1), picked, 0)
    width_full = grad_bins.shape[2]
    partial_value, gate_wgrad, up_wgrad, down_wgrad = expert_grads(
        inputs, grad_bins.reshape(experts * capacity, width_full), w_gate[0], w_up[0], w_down[0]
    )
    partial_value = partial_value.reshape(experts, capacity, width_full)
    returned = lax.all_to_all(partial_value, "expert", split_axis=0, concat_axis=0, tiled=True)
    summed = lax.psum_scatter(returned, ("dp", "tensor"), scatter_dimension=2, tiled=True)
    binned = summed.astype(jnp.bfloat16)
    features = binned.shape[2]
    padded_table = jnp.concatenate(
        [binned.reshape(experts * capacity, features), jnp.zeros((1, features), binned.dtype)],
        axis=0,
    )
    grad_input = jnp.take(padded_table, target, axis=0)
    return (grad_input, gate_wgrad[None], up_wgrad[None], down_wgrad[None])


def solution(mesh):
    placed = (
        P("expert", ("dp", "tensor")),
        P("expert"),
        P("expert"),
        P("expert"),
        P("expert", "dp", None),
        P("expert", None, None),
        P("expert", None),
        P("expert", None, ("dp", "tensor")),
        P("expert", None, ("dp", "tensor")),
        P("expert", ("dp", "tensor"), None),
    )
    return jax.shard_map(
        local,
        mesh=mesh,
        in_specs=placed,
        out_specs=(
            P("expert", ("dp", "tensor")),
            P("expert", None, ("dp", "tensor")),
            P("expert", None, ("dp", "tensor")),
            P("expert", ("dp", "tensor"), None),
        ),
        check_vma=False,
    )
```

profile of v0, /device:TPU:1, one launch (start us, length us, event | category | flops | bytes accessed | tf_op | source)
XLA Modules:
  0.0 363.5 jit_solution(7787104054758558859)
XLA Ops:
  7.2 0.7 all-gather.3.cloned.1.call-update
  8.0 0.7 all-gather.5.cloned.1.call-update
  8.7 0.7 compare_and_fusion.1
  9.4 56.7 %all-gather.3.cloned.1.call-done = bf16[512,2048]{1,0:T(8,128)(2,1)} async-done(((bf16[512,128]{1,0:T(8,128)(2,1)}), bf16[512,2048]{1,0:T(8,128)(2,1)}) %all-gather.3.cloned.1.call-update) | async-done | bytes 2097168 | tf_op jit(solution)/shard_map/all_gather | solution.py:69
  66.0 6.5 %scatter_custom_fusion = bf16[641,2048]{1,0:T(8,128)(2,1)} fusion(s32[512]{0:T(512)S(1)} %get-tuple-element.5, bf16[512,2048]{1,0:T(8,128)(2,1)} %all-gather.3.cloned.1.call-done, f32[512]{0:T(512)} %param.11, bf16[]{:T(256)} %constant.26.clone.1), kind=kCustom, calls=%fused_computation.12 | custom fusion | flops 3145728 | bytes 4724738 | tf_op jit(solution)/shard_map/scatter | solution.py:73
  72.6 3.6 slice.8
  76.2 8.7 %all-to-all-start = ((bf16[16,40,2048]{2,1,0:T(8,128)(2,1)}), bf16[16,40,2048]{2,1,0:T(8,128)(2,1)}, u32[]{:S(2)}, u32[]{:S(2)}) async-start(bf16[16,40,2048]{2,1,0:T(8,128)(2,1)} %bitcast.43), calls=%async_computation | async-start | bytes 5242880 | tf_op jit(solution)/shard_map/all_to_all | solution.py:75
  86.1 41.6 %all-gather.5.cloned.1.call-done = bf16[1,1280,2048]{2,1,0:T(8,128)(2,1)} async-done(((bf16[1,320,2048]{2,1,0:T(8,128)(2,1)}), bf16[1,1280,2048]{2,1,0:T(8,128)(2,1)}) %all-gather.5.cloned.1.call-update) | async-done | bytes 5242896 | tf_op jit(solution)/shard_map/all_gather | solution.py:82
  127.7 10.1 %gather_fusion = bf16[640,2048]{1,0:T(8,128)(2,1)} fusion(bf16[1280,2048]{1,0:T(8,128)(2,1)} %bitcast.41, s32[1024]{0:T(1024)S(1)} %pad_clamp_fusion.1), kind=kCustom, calls=%fused_computation | custom fusion | bytes 5245440 | tf_op jit(solution)/shard_map/jit(_take)/gather | solution.py:84
  137.8 2.1 select_select_fusion
  139.9 0.8 fusion.8
  141.9 1.7 fusion.11
  143.6 1.1 all-to-all-done
  144.8 3.2 multiply_convert_fusion.3
  148.0 0.9 fusion.6
  148.8 0.9 convolution_add_fusion
  149.8 124.9 %all_to_all.10 = f32[16,40,2048]{2,1,0:T(8,128)} all-to-all(f32[16,40,2048]{2,1,0:T(8,128)S(1)} %bitcast.42), channel_id=1, replica_groups=mesh['expert'=16,'dp'=4,'tensor'=4] {'expert'}, dimensions={0} | all-to-all | bytes 10485760 | tf_op jit(solution)/shard_map/all_to_all | solution.py:91
  274.7 3.9 %fusion.1 = bf16[1,2048,256]{2,1,0:T(8,128)(2,1)} fusion(bf16[640,2048]{1,0:T(8,128)(2,1)} %copy-done.1, bf16[640,256]{1,0:T(8,128)(2,1)S(1)} %get-tuple-element.6), kind=kOutput, calls=%fused_computation.10 | convolution fusion | flops 671612928 | bytes 3997696 | tf_op jit(solution)/shard_map/dot_general | solution.py:39
  278.6 2.0 fusion
  280.7 3.8 %fusion.2 = bf16[1,256,2048]{2,1,0:T(8,128)(2,1)} fusion(bf16[640,2048]{1,0:T(8,128)(2,1)} %bitcast.1, f32[640,256]{1,0:T(8,128)S(1)} %copy-done.4, f32[640,256]{1,0:T(8,128)S(1)} %fusion.8), kind=kOutput, calls=%fused_computation.11 | convolution fusion | flops 672595968 | bytes 4980736 | tf_op jit(solution)/shard_map/dot_general | solution.py:42
  284.5 69.3 %reduce-scatter.2.cloned.1.call-done = f32[16,40,128]{2,1,0:T(8,128)} async-done(((f32[16,40,2048]{2,1,0:T(8,128)}), f32[16,40,128]{2,1,0:T(8,128)}) %reduce-scatter.2.cloned.1.call-update) | async-done | bytes 327696 | tf_op jit(solution)/shard_map/reduce_scatter | solution.py:92
  353.8 1.0 convert_element_type.37
  354.8 1.3 gather_fusion.1
  356.2 0.8 broadcast_select_fusion
  (33 shorter events, 2.4 us)
Async XLA Ops:
  7.2 132.7 %copy-start = (bf16[1,2048,256]{2,1,0:T(8,128)(2,1)S(1)}, bf16[1,2048,256]{2,1,0:T(8,128)(2,1)}, u32[]{:S(2)}) copy-start(bf16[1,2048,256]{2,1,0:T(8,128)(2,1)} %param.17) | copy-start | bytes 3145732
  7.2 58.9 %all-gather.3.cloned.1.call-start = ((), (), s32[]{:S(2)}) async-start(), calls=%async_computation.3 | async-start | bytes 2228224 | tf_op jit(solution)/shard_map/all_gather | solution.py:69
  7.9 119.8 %all-gather.5.cloned.1.call-start = ((), (), s32[]{:S(2)}) async-start(), calls=%async_computation.4 | async-start | bytes 6553600 | tf_op jit(solution)/shard_map/all_gather | solution.py:82
  76.2 8.9 %copy-start.5 = (s32[1,16,40]{2,1,0:T(8,128)S(1)}, s32[1,16,40]{2,1,0:T(8,128)}, u32[]{:S(2)}) copy-start(s32[1,16,40]{2,1,0:T(8,128)} %param.15) | copy-start | bytes 7684
  76.2 9.1 %copy-start.6 = (s32[1,4]{1,0:T(1,128)S(1)}, s32[1,4]{1,0:T(1,128)}, u32[]{:S(2)}) copy-start(s32[1,4]{1,0:T(1,128)} %param.16) | copy-start | bytes 52
  76.2 68.6 %all-to-all-start = ((bf16[16,40,2048]{2,1,0:T(8,128)(2,1)}), bf16[16,40,2048]{2,1,0:T(8,128)(2,1)}, u32[]{:S(2)}, u32[]{:S(2)}) async-start(bf16[16,40,2048]{2,1,0:T(8,128)(2,1)} %bitcast.43), calls=%async_computation | async-start | bytes 5242880 | tf_op jit(solution)/shard_map/all_to_all | solution.py:75
  84.9 268.9 %reduce-scatter.2.cloned.1.call-start = ((), (), s32[]{:S(2)}) async-start(), calls=%async_computation.5 | async-start | bytes 5570560 | tf_op jit(solution)/shard_map/reduce_scatter | solution.py:92
  139.9 1.5 copy-start.1
  139.9 2.0 copy-start.3
  274.7 3.9 %copy-start.2 = (bf16[640,2048]{1,0:T(8,128)(2,1)S(1)}, bf16[640,2048]{1,0:T(8,128)(2,1)}, u32[]{:S(2)}) copy-start(bf16[640,2048]{1,0:T(8,128)(2,1)} %copy-done.1) | copy-start | bytes 7864324
  278.6 2.0 copy-start.4
Sparse Core Ops, SparseCore 0:
  10.4 55.5 all-gather.2
  67.9 59.7 all-gather.4
  274.8 78.9 reduce-scatter.1
where the time goes:
time: 364 us; the launch traced here: 363 us
  waiting for transfers between devices  170 us (47%)
  blocking collectives  125 us (34%)
  matrix products  17.2 us (5%)
  local copies, waits for them, and re-layouts  16.8 us (5%)
  between operations  13.9 us (4%)
  other arithmetic  11.5 us (3%)
  starting transfers between devices  8.99 us (2%)
    all_to_all x1, blocking collectives, local(): lax.all_to_all(partial_value, 'expert', split_axis=0, concat_axis=0, tile...  125 us
    reduce_scatter x1, waiting for transfers between devices, local(): lax.psum_scatter(returned, ('dp', 'tensor'), scatter_dimension=2, tiled=T...  69.3 us
    all_gather x1, waiting for transfers between devices, local(): full_rows = lax.all_gather(grad_out, ('dp', 'tensor'), axis=1, tiled=True)  56.7 us
    all_gather x1, waiting for transfers between devices, local(): stored = lax.all_gather(saved_rows, 'dp', axis=1, tiled=True)[0]  41.6 us
    gather x1, local copies, waits for them, and re-layouts, local(): picked = jnp.take(stored, row_index.reshape(-1), axis=0)  10.1 us
    all_to_all x1, starting transfers between devices, local(): lax.all_to_all(padded_table[:-1].reshape(experts, capacity, features), 'e...  8.7 us
  transfers between devices with their start and end apart: 4, of which 4 were waited for; matrix products, arithmetic and copies ran while one was open for 10% of the time, Pallas kernels for 0%

commit v1 on v0

v1 whole, which is shorter than its diff:
```python
import functools

import jax
import jax.numpy as jnp
from jax import lax
from jax.experimental import pallas as pl
from jax.experimental.pallas import tpu as pltpu
from jax.sharding import PartitionSpec as P

MESH = pl.DeviceIdType.MESH
BF16, F32 = jnp.bfloat16, jnp.float32
OFFSETS = (-2, 3, -3, 4, -4, 5, -5, 6, -6, 7, -7, 8, 0, 1, -1, 2)


def kernel(
    cap,
    blocks,
    grad_ref,
    prob_ref,
    ids_ref,
    slot_ref,
    saved_ref,
    rank_ref,
    counts_ref,
    gate_hbm,
    up_hbm,
    down_hbm,
    dinput_hbm,
    dgate_hbm,
    dup_hbm,
    ddown_hbm,
    w_gate,
    w_up,
    w_down,
    token_hot,
    row_hot,
    bin_send,
    bin_recv,
    saved_recv,
    x_all,
    g_all,
    hidden_all,
    both_all,
    part_send,
    part_recv,
    half_send,
    half_recv,
    back_send,
    back_recv,
    dgate_out,
    dup_out,
    ddown_out,
    dinput_out,
    local_sem,
    send_sem,
    recv_sem,
):
    experts = lax.axis_size("expert")
    me, mx, my = lax.axis_index("expert"), lax.axis_index("dp"), lax.axis_index("tensor")
    ring = lax.axis_size("dp")
    keep = saved_ref.shape[1]
    slots = experts * cap
    rows = slots // blocks
    per_block = experts // blocks
    half = rows // 2
    wide = bin_send.shape[1]
    chunk = grad_ref.shape[1]
    tokens = grad_ref.shape[0]

    started = []
    counter = [0]

    def remote(src, dst, device):
        number = counter[0]
        counter[0] += 1
        copy = pltpu.make_async_remote_copy(
            src_ref=src,
            dst_ref=dst,
            send_sem=send_sem.at[number],
            recv_sem=recv_sem.at[number],
            device_id=device,
            device_id_type=MESH,
        )
        copy.start()
        started.append(copy)
        return copy

    def xdev(step):
        return {"dp": lax.rem(mx + ring + step, ring)}

    def ydev(step):
        return {"tensor": lax.rem(my + ring + step, ring)}

    def edev(step):
        return {"expert": lax.rem(me + experts + step, experts)}

    loads = [
        pltpu.make_async_copy(gate_hbm.at[0], w_gate, local_sem.at[0]),
        pltpu.make_async_copy(up_hbm.at[0], w_up, local_sem.at[1]),
        pltpu.make_async_copy(down_hbm.at[0], w_down, local_sem.at[2]),
    ]
    own_saved = pltpu.make_async_copy(
        saved_ref.at[0, :, pl.ds(pl.multiple_of((mx * ring + my) * chunk, chunk), chunk)],
        saved_recv.at[mx],
        local_sem.at[3],
    )
    own_saved.start()

    barrier = pltpu.get_barrier_semaphore()
    greeted = 0
    for step in range(1, ring):
        pl.semaphore_signal(barrier, inc=1, device_id=xdev(step), device_id_type=MESH)
        pl.semaphore_signal(barrier, inc=1, device_id=ydev(step), device_id_type=MESH)
        greeted += 2
    for step in range(1, experts):
        pl.semaphore_signal(barrier, inc=1, device_id=edev(step), device_id_type=MESH)
        greeted += 1
    for load in loads:
        load.start()

    ids, slot = ids_ref[...], slot_ref[...]
    target = jnp.where(slot >= 0, ids * wide + slot, -1)
    place = lax.broadcasted_iota(jnp.int32, (experts * wide, tokens), 0)
    token_hot[...] = jnp.where(place == target, 1.0, 0.0).astype(BF16)
    prob = jnp.broadcast_to(prob_ref[...], (chunk, tokens)).T
    scaled = (prob * grad_ref[...].astype(F32)).astype(BF16)
    bins = jnp.dot(token_hot[...], scaled, preferred_element_type=F32)
    bin_send[...] = bins.astype(BF16).reshape(experts, wide, chunk)

    pl.semaphore_wait(barrier, greeted)

    saved_copies = []
    for step in (2, 1, 3):
        to = lax.rem(mx + step, ring)
        columns = pl.ds(pl.multiple_of((to * ring + my) * chunk, chunk), chunk)
        saved_copies.append(
            remote(saved_ref.at[0, :, columns], saved_recv.at[mx], {"dp": to})
        )
    bin_copies = {}
    for spot, offset in enumerate(OFFSETS):
        if offset != 0:
            to = lax.rem(me + experts - offset, experts)
            bin_copies[spot] = remote(bin_send.at[to], bin_recv.at[spot], {"expert": to})

    lane = lax.broadcasted_iota(jnp.int32, (1, ring * keep), 1)
    position = jnp.full((1, ring * keep), -2, jnp.int32)
    before = jnp.int32(0)
    for part in range(ring):
        count = counts_ref[0, part]
        inside = (lane >= part * keep) & (lane < part * keep + count)
        position = jnp.where(inside, lane - part * keep + before, position)
        before = before + count
    position = position.astype(F32)
    diagonal = lax.broadcasted_iota(jnp.int32, (cap, cap), 0) == lax.broadcasted_iota(
        jnp.int32, (cap, cap), 1
    )
    for block in range(blocks):
        parts = []
        for spot in range(block * per_block, (block + 1) * per_block):
            group = lax.rem(me + experts + OFFSETS[spot], experts)
            rank = rank_ref[0, pl.ds(group, 1), :].astype(F32)
            column = jnp.sum(jnp.where(diagonal, rank, 0.0), axis=1, keepdims=True)
            parts.append(jnp.where(column == position, 1.0, 0.0))
        row_hot[pl.ds(block * rows, rows), :] = jnp.concatenate(parts, axis=0).astype(BF16)

    own_saved.wait()
    for copy in saved_copies:
        copy.wait_recv()

    x_first, g_first = {}, {}
    stored = saved_recv[...].reshape(ring * keep, chunk)
    for block in range(blocks):
        span = pl.ds(block * rows, rows)
        x_all[mx, my, span, :] = jnp.dot(
            row_hot[span, :], stored, preferred_element_type=F32
        ).astype(BF16)
        x_first[block] = [
            remote(x_all.at[mx, my, span], x_all.at[mx, my, span], xdev(step)) for step in (2, 1, 3)
        ]
    for block in range(blocks):
        span = pl.ds(block * rows, rows)
        parts = []
        for spot in range(block * per_block, (block + 1) * per_block):
            if OFFSETS[spot] == 0:
                piece = bin_send[me]
            else:
                bin_copies[spot].wait_recv()
                piece = bin_recv[spot]
            parts.append(piece.astype(F32)[:cap])
        g_all[mx, my, span, :] = jnp.concatenate(parts, axis=0).astype(BF16)
        g_first[block] = [
            remote(g_all.at[mx, my, span], g_all.at[mx, my, span], ydev(step)) for step in (2, 1, 3)
        ]

    near, far = {}, {}

    def spread(block):
        span = pl.ds(block * rows, rows)
        for copy in x_first[block]:
            copy.wait_recv()
        piece = x_all.at[:, my, span]
        x_near = [remote(piece, piece, ydev(1)), remote(piece, piece, ydev(-1))]
        for copy in g_first[block]:
            copy.wait_recv()
        piece = g_all.at[mx, :, span]
        g_near = [remote(piece, piece, xdev(1)), remote(piece, piece, xdev(-1))]
        near[block] = (x_near, g_near)

    def forward(block):
        span = pl.ds(block * rows, rows)
        low, high = lax.rem(my + ring - 1, ring), lax.rem(my + 1, ring)
        x_near, g_near = near[block]
        x_near[0].wait_recv()
        piece = x_all.at[pl.ds(0, ring // 2), low, span]
        copies = [remote(piece, piece, ydev(1))]
        x_near[1].wait_recv()
        piece = x_all.at[pl.ds(ring // 2, ring // 2), high, span]
        copies.append(remote(piece, piece, ydev(-1)))
        low, high = lax.rem(mx + ring - 1, ring), lax.rem(mx + 1, ring)
        g_near[0].wait_recv()
        piece = g_all.at[low, pl.ds(0, ring // 2), span]
        copies.append(remote(piece, piece, xdev(1)))
        g_near[1].wait_recv()
        piece = g_all.at[high, pl.ds(ring // 2, ring // 2), span]
        copies.append(remote(piece, piece, xdev(-1)))
        far[block] = copies

    part_copies, half_copies, back_copies = {}, {}, {}

    def compute(block):
        span = pl.ds(block * rows, rows)
        for copy in far[block]:
            copy.wait_recv()
        inputs = jnp.concatenate(
            [x_all[c // ring, c % ring, span, :] for c in range(ring * ring)], axis=1
        )
        gate_pre = jnp.dot(inputs, w_gate[...], preferred_element_type=F32)
        up_pre = jnp.dot(inputs, w_up[...], preferred_element_type=F32)
        grads = jnp.concatenate(
            [g_all[c // ring, c % ring, span, :] for c in range(ring * ring)], axis=1
        )
        hidden_grad = lax.dot_general(
            grads, w_down[...], (((1,), (1,)), ((), ())), preferred_element_type=F32
        )
        squash = 1.0 / (1.0 + jnp.exp(-gate_pre))
        activated = gate_pre * squash
        hidden_all[span, :] = (activated * up_pre).astype(BF16)
        up_grad = (hidden_grad * activated).astype(BF16)
        gate_grad = (hidden_grad * up_pre * squash * (1.0 + gate_pre * (1.0 - squash))).astype(BF16)
        units = gate_grad.shape[1]
        both_all[span, pl.ds(0, units)] = gate_grad
        both_all[span, pl.ds(units, units)] = up_grad
        for x in range(ring):
            piece = pl.ds(x * ring * chunk, ring * chunk)
            total = lax.dot_general(
                gate_grad, w_gate[piece, :], (((1,), (1,)), ((), ())), preferred_element_type=F32
            ) + lax.dot_general(
                up_grad, w_up[piece, :], (((1,), (1,)), ((), ())), preferred_element_type=F32
            )
            total = total.astype(BF16)
            for y in range(ring):
                part_send[block, x, y] = total[:, y * chunk : (y + 1) * chunk]
        first, second = pl.ds(0, half), pl.ds(half, half)
        copies = []
        for step in (2, 1, 3):
            to = lax.rem(mx + step, ring)
            copies.append(
                remote(
                    part_send.at[block, to, :, first],
                    part_recv.at[block, 0, step - 1],
                    {"dp": to},
                )
            )
            to = lax.rem(my + step, ring)
            copies.append(
                remote(
                    part_send.at[block, :, to, second],
                    part_recv.at[block, 1, step - 1],
                    {"tensor": to},
                )
            )
        part_copies[block] = copies

    def reduce_first(block):
        first, second = pl.ds(0, half), pl.ds(half, half)
        copies = part_copies[block]
        for copy in copies[0::2]:
            copy.wait_recv()
        total = part_send[block, mx, :, first, :].astype(F32)
        for step in range(ring - 1):
            total = total + part_recv[block, 0, step].astype(F32)
        half_send[block, 0] = total.astype(BF16)
        sent = []
        for step in (2, 1, 3):
            to = lax.rem(my + step, ring)
            sent.append(
                remote(half_send.at[block, 0, to], half_recv.at[block, 0, step - 1], {"tensor": to})
            )
        for copy in copies[1::2]:
            copy.wait_recv()
        total = part_send[block, :, my, second, :].astype(F32)
        for step in range(ring - 1):
            total = total + part_recv[block, 1, step].astype(F32)
        half_send[block, 1] = total.astype(BF16)
        for step in (2, 1, 3):
            to = lax.rem(mx + step, ring)
            sent.append(
                remote(half_send.at[block, 1, to], half_recv.at[block, 1, step - 1], {"dp": to})
            )
        half_copies[block] = sent

    def reduce_second(block):
        spare = jnp.zeros((wide - cap, chunk), F32)
        for which, own in ((0, my), (1, mx)):
            for copy in half_copies[block][3 * which : 3 * which + 3]:
                copy.wait_recv()
            total = half_send[block, which, own].astype(F32)
            for step in range(ring - 1):
                total = total + half_recv[block, which, step].astype(F32)
            for inner in range(per_block // 2):
                spot = block * per_block + which * (per_block // 2) + inner
                piece = jnp.concatenate([total[inner * cap : (inner + 1) * cap], spare], axis=0)
                if OFFSETS[spot] == 0:
                    back_recv[me] = piece.astype(BF16)
                else:
                    back_send[spot] = piece.astype(BF16)
                    to = lax.rem(me + experts + OFFSETS[spot], experts)
                    back_copies[spot] = remote(
                        back_send.at[spot], back_recv.at[me], {"expert": to}
                    )

    outs = []

    def store(src, dst, number):
        copy = pltpu.make_async_copy(src, dst, local_sem.at[number])
        copy.start()
        outs.append(copy)

    def weight_grads_in():
        units = w_gate.shape[1]
        for c in range(ring * ring):
            both = lax.dot_general(
                x_all[c // ring, c % ring],
                both_all[...],
                (((0,), (0,)), ((), ())),
                preferred_element_type=F32,
            ).astype(BF16)
            dgate_out[pl.ds(c * chunk, chunk), :] = both[:, :units]
            dup_out[pl.ds(c * chunk, chunk), :] = both[:, units:]
        store(dgate_out, dgate_hbm.at[0], 4)
        store(dup_out, dup_hbm.at[0], 5)

    def weight_grads_out():
        hidden = hidden_all[...].astype(F32).T.astype(BF16)
        for c in range(0, ring * ring, 2):
            pair = jnp.concatenate(
                [g_all[c // ring, c % ring], g_all[(c + 1) // ring, (c + 1) % ring]], axis=1
            )
            ddown_out[:, pl.ds(c * chunk, 2 * chunk)] = jnp.dot(
                hidden, pair, preferred_element_type=F32
            ).astype(BF16)
        store(ddown_out, ddown_hbm.at[0], 6)

    for load in loads:
        load.wait()
    spread(0)
    for block in range(blocks + 3):
        if block + 1 < blocks:
            spread(block + 1)
        if block < blocks:
            forward(block)
        if 0 <= block - 1 < blocks:
            compute(block - 1)
        if 0 <= block - 2 < blocks:
            if block - 2 == blocks - 1:
                weight_grads_in()
            reduce_first(block - 2)
        if 0 <= block - 3 < blocks:
            if block - 3 == blocks - 1:
                weight_grads_out()
            reduce_second(block - 3)

    for copy in back_copies.values():
        copy.wait_recv()
    returned = back_recv[...].reshape(experts * wide, chunk)
    dinput_out[...] = lax.dot_general(
        token_hot[...], returned, (((0,), (0,)), ((), ())), preferred_element_type=F32
    ).astype(BF16)
    store(dinput_out, dinput_hbm, 7)
    for copy in started:
        copy.wait_send()
    for copy in outs:
        copy.wait()


def local(
    grad_out,
    gate_prob,
    expert_ids,
    slot_index,
    saved_rows,
    row_rank,
    part_counts,
    w_gate,
    w_up,
    w_down,
):
    experts, cap = row_rank.shape[1], row_rank.shape[2]
    tokens, chunk = grad_out.shape
    ring = part_counts.shape[1]
    keep = saved_rows.shape[1]
    width, units = w_gate.shape[1], w_gate.shape[2]
    blocks = 4
    slots = experts * cap
    rows = slots // blocks
    wide = 48
    copies = 2 * (experts - 1) + 3 + blocks * (6 + 8 + 12)
    vmem = pl.BlockSpec(memory_space=pltpu.VMEM)
    anywhere = pl.BlockSpec(memory_space=pl.ANY)
    return pl.pallas_call(
        functools.partial(kernel, cap, blocks),
        out_shape=(
            jax.ShapeDtypeStruct((tokens, chunk), BF16),
            jax.ShapeDtypeStruct(w_gate.shape, BF16),
            jax.ShapeDtypeStruct(w_up.shape, BF16),
            jax.ShapeDtypeStruct(w_down.shape, BF16),
        ),
        in_specs=[
            vmem,
            vmem,
            vmem,
            vmem,
            anywhere,
            vmem,
            pl.BlockSpec(memory_space=pltpu.SMEM),
            anywhere,
            anywhere,
            anywhere,
        ],
        out_specs=(anywhere,) * 4,
        scratch_shapes=[
            pltpu.VMEM((width, units), BF16),
            pltpu.VMEM((width, units), BF16),
            pltpu.VMEM((units, width), BF16),
            pltpu.VMEM((experts * wide, tokens), BF16),
            pltpu.VMEM((slots, ring * keep), BF16),
            pltpu.VMEM((experts, wide, chunk), BF16),
            pltpu.VMEM((experts, wide, chunk), BF16),
            pltpu.VMEM((ring, keep, chunk), BF16),
            pltpu.VMEM((ring, ring, slots, chunk), BF16),
            pltpu.VMEM((ring, ring, slots, chunk), BF16),
            pltpu.VMEM((slots, units), BF16),
            pltpu.VMEM((slots, 2 * units), BF16),
            pltpu.VMEM((blocks, ring, ring, rows, chunk), BF16),
            pltpu.VMEM((blocks, 2, ring - 1, ring, rows // 2, chunk), BF16),
            pltpu.VMEM((blocks, 2, ring, rows // 2, chunk), BF16),
            pltpu.VMEM((blocks, 2, ring - 1, rows // 2, chunk), BF16),
            pltpu.VMEM((experts, wide, chunk), BF16),
            pltpu.VMEM((experts, wide, chunk), BF16),
            pltpu.VMEM((width, units), BF16),
            pltpu.VMEM((width, units), BF16),
            pltpu.VMEM((units, width), BF16),
            pltpu.VMEM((tokens, chunk), BF16),
            pltpu.SemaphoreType.DMA((8,)),
            pltpu.SemaphoreType.DMA((copies,)),
            pltpu.SemaphoreType.DMA((copies,)),
        ],
        compiler_params=pltpu.CompilerParams(
            collective_id=0, has_side_effects=True, vmem_limit_bytes=56 << 20
        ),
        name="experts_backward",
    )(
        grad_out,
        gate_prob.reshape(1, tokens),
        expert_ids.reshape(1, tokens),
        slot_index.reshape(1, tokens),
        saved_rows,
        row_rank,
        part_counts,
        w_gate,
        w_up,
        w_down,
    )


def solution(mesh):
    placed = (
        P("expert", ("dp", "tensor")),
        P("expert"),
        P("expert"),
        P("expert"),
        P("expert", "dp", None),
        P("expert", None, None),
        P("expert", None),
        P("expert", None, ("dp", "tensor")),
        P("expert", None, ("dp", "tensor")),
        P("expert", ("dp", "tensor"), None),
    )
    return jax.shard_map(
        local,
        mesh=mesh,
        in_specs=placed,
        out_specs=(
            P("expert", ("dp", "tensor")),
            P("expert", None, ("dp", "tensor")),
            P("expert", None, ("dp", "tensor")),
            P("expert", ("dp", "tensor"), None),
        ),
        check_vma=False,
    )
```

time: 364 us -> 83.3 us (0.23)
  waiting for transfers between devices: 170 us -> 0 us
  blocking collectives: 125 us -> 0 us
  Pallas kernels: 0 us -> 75.9 us
  matrix products: 17.2 us -> 0 us
  between operations: 13.9 us -> 0.65 us
  other arithmetic: 11.5 us -> 0 us
  local copies, waits for them, and re-layouts: 16.8 us -> 6.49 us
  starting transfers between devices: 8.99 us -> 0 us
    all_to_all x1 -> x0, blocking collectives: 125 us -> none  [local(): lax.all_to_all(partial_value, 'expert', split_axis=0, concat_axis=0, tile...]
    all_gather x2 -> x0, waiting for transfers between devices: 98.3 us -> none  [the longest x1 56.7 us: local(): full_rows = lax.all_gather(grad_out, ('dp', 'tensor'), axis=1, tiled=True)]
    pallas_call x0 -> x1, Pallas kernels: none -> 75.9 us  [local(): pl.pallas_call(functools.partial(kernel, cap, blocks), out_shape=(jax.Sha...]
    reduce_scatter x1 -> x0, waiting for transfers between devices: 69.3 us -> none  [local(): lax.psum_scatter(returned, ('dp', 'tensor'), scatter_dimension=2, tiled=T...]
    dot_general x8 -> x0, matrix products: 17.2 us -> none  [the longest x1 3.9 us: expert_grads(): lax.dot_general(inputs, up_grad, (((0,), (0,)), ((), ())), preferred_elem...]
    gather x2 -> x0, local copies, waits for them, and re-layouts: 11.4 us -> none  [the longest x1 10.1 us: local(): picked = jnp.take(stored, row_index.reshape(-1), axis=0)]
    all_to_all x1 -> x0, starting transfers between devices: 8.7 us -> none  [local(): lax.all_to_all(padded_table[:-1].reshape(experts, capacity, features), 'e...]
    scatter x1 -> x0, other arithmetic: 6.5 us -> none  [local(): jnp.zeros((experts * capacity + 1, features), scaled.dtype).at[target]]
  transfers between devices with their start and end apart: 4 -> 0, of which waited for: 4 -> 0; matrix products, arithmetic and copies ran while one was open for 10% -> 0% of each run, Pallas kernels for 0% -> 0%
where the time goes in v1:
time: 83.3 us; the launch traced here: 83.1 us
  Pallas kernels  75.9 us (91%)
  local copies, waits for them, and re-layouts  6.49 us (8%)
    pallas_call x1, Pallas kernels, local(): pl.pallas_call(functools.partial(kernel, cap, blocks), out_shape=(jax.Sha...  75.9 us
    unnamed x8, local copies, waits for them, and re-layouts  6.49 us

profile of v1, /device:TPU:1, one launch (start us, length us, event | category | flops | bytes accessed | tf_op | source)
XLA Modules:
  0.0 83.1 jit_solution(1601427180850365648)
XLA Ops:
  0.6 75.9 %experts_backward.1 = (bf16[512,128]{1,0:T(8,128)(2,1)}, bf16[1,2048,256]{2,1,0:T(8,128)(2,1)}, bf16[1,2048,256]{2,1,0:T(8,128)(2,1)}, bf16[1,256,2048]{2,1,0:T(8,128)(2,1)}) custom-call(bf16[512,128]{1,0:T(8,128)(2,1)} %grad_ref.1, f32[1,512]{1,0:T(1,128)} %bitcast.3, s32[1,512]{1,0:T(1,128)} %bitcast.4, s32[1,512]{1,0:T(1,128)} %bitcast.5, ...), custom_call_target="tpu_custom_call" | custom-call | tf_op jit(solution)/shard_map/experts_backward/pallas_call | solution.py:420
  76.6 0.0 copy-start.1
  76.6 1.7 %copy.18 = bf16[512,128]{1,0:T(8,128)(2,1)} copy(bf16[512,128]{1,0:T(8,128)(2,1)} %get-tuple-element.8) | data formatting | bytes 262144
  78.2 2.3 %copy.19 = bf16[1,2048,256]{2,1,0:T(8,128)(2,1)} copy(bf16[1,2048,256]{2,1,0:T(8,128)(2,1)} %get-tuple-element.9) | data formatting | bytes 2097152
  80.5 0.0 copy-done.1
  80.5 0.0 copy-start
  80.5 1.0 %copy.20 = bf16[1,2048,256]{2,1,0:T(8,128)(2,1)} copy(bf16[1,2048,256]{2,1,0:T(8,128)(2,1)S(1)} %copy-done.1) | data formatting | bytes 2097152
  81.5 0.6 copy-done
  82.1 1.0 %copy.21 = bf16[1,256,2048]{2,1,0:T(8,128)(2,1)} copy(bf16[1,256,2048]{2,1,0:T(8,128)(2,1)S(1)} %copy-done) | data formatting | bytes 2097152
Async XLA Ops:
  76.6 3.9 %copy-start.1 = (bf16[1,2048,256]{2,1,0:T(8,128)(2,1)S(1)}, bf16[1,2048,256]{2,1,0:T(8,128)(2,1)}, u32[]{:S(2)}) copy-start(bf16[1,2048,256]{2,1,0:T(8,128)(2,1)} %get-tuple-element.10) | copy-start | bytes 3145732
  80.5 1.6 %copy-start = (bf16[1,256,2048]{2,1,0:T(8,128)(2,1)S(1)}, bf16[1,256,2048]{2,1,0:T(8,128)(2,1)}, u32[]{:S(2)}) copy-start(bf16[1,256,2048]{2,1,0:T(8,128)(2,1)} %get-tuple-element.11) | copy-start | bytes 3145732

commit v2 on v1

v2 whole, which is shorter than its diff:
```python
import functools

import jax
import jax.numpy as jnp
from jax import lax
from jax.experimental import pallas as pl
from jax.experimental.pallas import tpu as pltpu
from jax.sharding import PartitionSpec as P

MESH = pl.DeviceIdType.MESH
BF16, F32 = jnp.bfloat16, jnp.float32
BLOCKS = (4, 4, 4, 4)
DIRECT_SHARES = 1
DIRECT_SUMS = 1
OFFSETS = (-2, 3, -3, 4, -4, 5, -5, 6, -6, 7, -7, 8, 0, 1, -1, 2)


def kernel(
    cap,
    grad_hbm,
    prob_hbm,
    ids_hbm,
    slot_hbm,
    saved_ref,
    rank_hbm,
    counts_hbm,
    gate_hbm,
    up_hbm,
    down_hbm,
    dinput_out,
    dgate_out,
    dup_out,
    ddown_out,
    grad_ref,
    prob_ref,
    ids_ref,
    slot_ref,
    rank_ref,
    counts_ref,
    w_gate,
    w_up,
    w_down,
    token_hot,
    row_hot,
    bin_send,
    bin_recv,
    saved_recv,
    x_all,
    g_all,
    hidden_all,
    both_all,
    part_send,
    fold_recv,
    part_recv,
    half_send,
    half_recv,
    back_send,
    back_recv,
    local_sem,
    send_sem,
    recv_sem,
):
    experts = lax.axis_size("expert")
    me, mx, my = lax.axis_index("expert"), lax.axis_index("dp"), lax.axis_index("tensor")
    ring = lax.axis_size("dp")
    keep = saved_ref.shape[1]
    wide = bin_send.shape[1]
    tokens, chunk = grad_ref.shape
    units = w_gate.shape[1]
    last = len(BLOCKS) - 1
    first_group = [sum(BLOCKS[:block]) for block in range(len(BLOCKS))]

    def rows_of(block):
        return first_group[block] * cap, BLOCKS[block] * cap

    def span_of(block):
        return pl.ds(*rows_of(block))

    def halves_of(block):
        start, size = rows_of(block)
        cut = size // 32 * 16
        return (pl.ds(start, cut), pl.ds(start + cut, size - cut))

    started = []

    def remote(src, dst, device):
        number = len(started)
        copy = pltpu.make_async_remote_copy(
            src_ref=src,
            dst_ref=dst,
            send_sem=send_sem.at[number],
            recv_sem=recv_sem.at[number],
            device_id=device,
            device_id_type=MESH,
        )
        copy.start()
        started.append(copy)
        return copy

    def xdev(step):
        return {"dp": lax.rem(mx + ring + step, ring)}

    def ydev(step):
        return {"tensor": lax.rem(my + ring + step, ring)}

    def edev(step):
        return {"expert": lax.rem(me + experts + step, experts)}

    small = [
        pltpu.make_async_copy(src, dst, local_sem.at[number])
        for number, (src, dst) in enumerate(
            (
                (grad_hbm, grad_ref),
                (prob_hbm, prob_ref),
                (ids_hbm, ids_ref),
                (slot_hbm, slot_ref),
                (rank_hbm.at[0], rank_ref),
                (counts_hbm, counts_ref),
                (
                    saved_ref.at[0, :, pl.ds(pl.multiple_of((mx * ring + my) * chunk, chunk), chunk)],
                    saved_recv.at[mx],
                ),
            )
        )
    ]
    loads = [
        pltpu.make_async_copy(src.at[0], dst, local_sem.at[len(small) + number])
        for number, (src, dst) in enumerate(((gate_hbm, w_gate), (up_hbm, w_up), (down_hbm, w_down)))
    ]
    for load in small:
        load.start()

    barrier = pltpu.get_barrier_semaphore()
    greeted = 0
    for step in range(1, ring):
        pl.semaphore_signal(barrier, inc=1, device_id=xdev(step), device_id_type=MESH)
        pl.semaphore_signal(barrier, inc=1, device_id=ydev(step), device_id_type=MESH)
        greeted += 2
    for step in range(1, experts):
        pl.semaphore_signal(barrier, inc=1, device_id=edev(step), device_id_type=MESH)
        greeted += 1
    for load in loads:
        load.start()
    for load in small:
        load.wait()

    ids, slot = ids_ref[...], slot_ref[...]
    target = jnp.where(slot >= 0, ids * wide + slot, -1)
    place = lax.broadcasted_iota(jnp.int32, (experts * wide, tokens), 0)
    token_hot[...] = jnp.where(place == target, 1.0, 0.0).astype(BF16)
    prob = jnp.broadcast_to(prob_ref[...], (chunk, tokens)).T
    scaled = (prob * grad_ref[...].astype(F32)).astype(BF16)
    bins = jnp.dot(token_hot[...], scaled, preferred_element_type=F32)
    bin_send[...] = bins.astype(BF16).reshape(experts, wide, chunk)

    pl.semaphore_wait(barrier, greeted)

    saved_copies = []
    for step in (2, 1, 3):
        to = lax.rem(mx + step, ring)
        columns = pl.ds(pl.multiple_of((to * ring + my) * chunk, chunk), chunk)
        saved_copies.append(
            remote(saved_ref.at[0, :, columns], saved_recv.at[mx], {"dp": to})
        )
    bin_copies = {}
    for spot, offset in enumerate(OFFSETS):
        if offset != 0:
            to = lax.rem(me + experts - offset, experts)
            bin_copies[spot] = remote(bin_send.at[to], bin_recv.at[spot], {"expert": to})

    lane = lax.broadcasted_iota(jnp.int32, (1, ring * keep), 1)
    position = jnp.full((1, ring * keep), -2, jnp.int32)
    before = jnp.zeros((1, 1), jnp.int32)
    for part in range(ring):
        count = counts_ref[:, part : part + 1]
        inside = (lane >= part * keep) & (lane < part * keep + count)
        position = jnp.where(inside, lane - part * keep + before, position)
        before = before + count
    position = position.astype(F32)
    diagonal = lax.broadcasted_iota(jnp.int32, (cap, cap), 0) == lax.broadcasted_iota(
        jnp.int32, (cap, cap), 1
    )
    for block in range(len(BLOCKS)):
        parts = []
        for spot in range(first_group[block], first_group[block] + BLOCKS[block]):
            group = lax.rem(me + experts + OFFSETS[spot], experts)
            rank = rank_ref[pl.ds(group, 1), :].astype(F32)
            column = jnp.sum(jnp.where(diagonal, rank, 0.0), axis=1, keepdims=True)
            parts.append(jnp.where(column == position, 1.0, 0.0))
        row_hot[span_of(block), :] = jnp.concatenate(parts, axis=0).astype(BF16)

    x_first, g_first = {}, {}

    def share(block, ref, device):
        piece = ref.at[mx, my, span_of(block)]
        return [remote(piece, piece, device(step)) for step in ((2, 1, 3) if block < DIRECT_SHARES else (1, 3))]

    def pick_x(block):
        if block == 0:
            for copy in saved_copies:
                copy.wait_recv()
        span = span_of(block)
        x_all[mx, my, span, :] = jnp.dot(
            row_hot[span, :], saved_recv[...].reshape(ring * keep, chunk), preferred_element_type=F32
        ).astype(BF16)
        x_first[block] = share(block, x_all, xdev)

    def pick_g(block):
        parts = []
        for spot in range(first_group[block], first_group[block] + BLOCKS[block]):
            if OFFSETS[spot] == 0:
                piece = bin_send[me]
            else:
                bin_copies[spot].wait_recv()
                piece = bin_recv[spot]
            parts.append(piece.astype(F32)[:cap])
        g_all[mx, my, span_of(block), :] = jnp.concatenate(parts, axis=0).astype(BF16)
        g_first[block] = share(block, g_all, ydev)

    low_x, high_x = lax.rem(mx + ring - 1, ring), lax.rem(mx + 1, ring)
    low_y, high_y = lax.rem(my + ring - 1, ring), lax.rem(my + 1, ring)

    def relay(block):
        if block < DIRECT_SHARES:
            return
        first, second = halves_of(block)
        for copies, ref, low, high, device in (
            (x_first, x_all, (low_x, my), (high_x, my), xdev),
            (g_first, g_all, (mx, low_y), (mx, high_y), ydev),
        ):
            up, down = copies[block]
            up.wait_recv()
            piece = ref.at[low[0], low[1], first]
            sent = [remote(piece, piece, device(1))]
            down.wait_recv()
            piece = ref.at[high[0], high[1], second]
            sent.append(remote(piece, piece, device(-1)))
            copies[block] = sent

    near, far = {}, {}

    def spread(block):
        span = span_of(block)
        for copy in x_first[block]:
            copy.wait_recv()
        piece = x_all.at[:, my, span]
        x_near = [remote(piece, piece, ydev(1)), remote(piece, piece, ydev(-1))]
        for copy in g_first[block]:
            copy.wait_recv()
        piece = g_all.at[mx, :, span]
        g_near = [remote(piece, piece, xdev(1)), remote(piece, piece, xdev(-1))]
        near[block] = (x_near, g_near)

    low_half, high_half = pl.ds(0, ring // 2), pl.ds(ring // 2, ring // 2)

    def forward(block):
        span = span_of(block)
        x_near, g_near = near[block]
        x_near[0].wait_recv()
        piece = x_all.at[low_half, low_y, span]
        copies = [remote(piece, piece, ydev(1))]
        x_near[1].wait_recv()
        piece = x_all.at[high_half, high_y, span]
        copies.append(remote(piece, piece, ydev(-1)))
        g_near[0].wait_recv()
        piece = g_all.at[low_x, low_half, span]
        copies.append(remote(piece, piece, xdev(1)))
        g_near[1].wait_recv()
        piece = g_all.at[high_x, high_half, span]
        copies.append(remote(piece, piece, xdev(-1)))
        far[block] = copies

    def along(which, index, others, span):
        return part_send.at[(index, others, span) if which == 0 else (others, index, span)]

    lines = (
        (xdev, mx, low_x, high_x, ydev, my),
        (ydev, my, low_y, high_y, xdev, mx),
    )
    part_copies, half_copies, back_copies = {}, {}, {}

    def compute(block):
        span = span_of(block)
        for copy in far[block]:
            copy.wait_recv()
        inputs = jnp.concatenate(
            [x_all[c // ring, c % ring, span, :] for c in range(ring * ring)], axis=1
        )
        gate_pre = jnp.dot(inputs, w_gate[...], preferred_element_type=F32)
        up_pre = jnp.dot(inputs, w_up[...], preferred_element_type=F32)
        grads = jnp.concatenate(
            [g_all[c // ring, c % ring, span, :] for c in range(ring * ring)], axis=1
        )
        hidden_grad = lax.dot_general(
            grads, w_down[...], (((1,), (1,)), ((), ())), preferred_element_type=F32
        )
        squash = 1.0 / (1.0 + jnp.exp(-gate_pre))
        activated = gate_pre * squash
        hidden_all[span, :] = (activated * up_pre).astype(BF16)
        up_grad = (hidden_grad * activated).astype(BF16)
        gate_grad = (hidden_grad * up_pre * squash * (1.0 + gate_pre * (1.0 - squash))).astype(BF16)
        both_all[span, pl.ds(0, units)] = gate_grad
        both_all[span, pl.ds(units, units)] = up_grad
        for x in range(ring):
            piece = pl.ds(x * ring * chunk, ring * chunk)
            total = lax.dot_general(
                gate_grad, w_gate[piece, :], (((1,), (1,)), ((), ())), preferred_element_type=F32
            ) + lax.dot_general(
                up_grad, w_up[piece, :], (((1,), (1,)), ((), ())), preferred_element_type=F32
            )
            total = total.astype(BF16)
            for y in range(ring):
                part_send[x, y, span, :] = total[:, y * chunk : (y + 1) * chunk]
        copies = [[], []]
        for which, span in enumerate(halves_of(block)):
            device, mine, low, high = lines[which][:4]
            if block > last - DIRECT_SUMS:
                for step in (2, 1, 3):
                    to = lax.rem(mine + step, ring)
                    copies[which].append(
                        remote(
                            along(which, to, slice(None), span),
                            part_recv.at[step - 1, :, span],
                            device(step),
                        )
                    )
                continue
            other = lax.rem(mine + 2, ring)
            copies[which] = [
                remote(along(which, other, low_half, span), fold_recv.at[0, :, span], device(1)),
                remote(along(which, other, high_half, span), fold_recv.at[1, :, span], device(-1)),
                remote(
                    along(which, high, high_half, span), part_recv.at[0, high_half, span], device(1)
                ),
                remote(
                    along(which, low, low_half, span), part_recv.at[1, low_half, span], device(-1)
                ),
            ]
        part_copies[block] = copies

    def fold(block):
        if block > last - DIRECT_SUMS:
            return
        for which, span in enumerate(halves_of(block)):
            device, mine, low, high = lines[which][:4]
            copies = part_copies[block][which]
            for number, (index, others, step) in enumerate(
                ((high, low_half, 1), (low, high_half, -1))
            ):
                copies[number].wait_recv()
                piece = along(which, index, others, span)
                piece[...] = (
                    piece[...].astype(F32) + fold_recv[number, :, span, :].astype(F32)
                ).astype(BF16)
                copies.append(remote(piece, part_recv.at[number, others, span], device(step)))
            part_copies[block][which] = copies[2:]

    def reduce_first(block):
        sent = [[], []]
        for which, span in enumerate(halves_of(block)):
            mine = lines[which][1]
            device, own = lines[which][4:]
            for copy in part_copies[block][which]:
                copy.wait_recv()
            total = along(which, mine, slice(None), span)[...].astype(F32)
            for step in range(ring - 1 if block > last - DIRECT_SUMS else 2):
                total = total + part_recv[step, :, span, :].astype(F32)
            half_send[:, span, :] = total.astype(BF16)
            for step in (2, 1, 3):
                to = lax.rem(own + step, ring)
                sent[which].append(
                    remote(half_send.at[to, span], half_recv.at[step - 1, span], device(step))
                )
        half_copies[block] = sent

    def reduce_second(block):
        spare = jnp.zeros((wide - cap, chunk), F32)
        totals = []
        for which, span in enumerate(halves_of(block)):
            own = lines[which][5]
            for copy in half_copies[block][which]:
                copy.wait_recv()
            total = half_send[own, span, :].astype(F32)
            for step in range(ring - 1):
                total = total + half_recv[step, span, :].astype(F32)
            totals.append(total)
        total = jnp.concatenate(totals, axis=0)
        for inner in range(BLOCKS[block]):
            spot = first_group[block] + inner
            piece = jnp.concatenate([total[inner * cap : (inner + 1) * cap], spare], axis=0)
            if OFFSETS[spot] == 0:
                back_recv[me] = piece.astype(BF16)
            else:
                back_send[spot] = piece.astype(BF16)
                back_copies[spot] = remote(
                    back_send.at[spot], back_recv.at[me], edev(OFFSETS[spot])
                )

    def weight_grads_in():
        for c in range(ring * ring):
            both = lax.dot_general(
                x_all[c // ring, c % ring],
                both_all[...],
                (((0,), (0,)), ((), ())),
                preferred_element_type=F32,
            ).astype(BF16)
            dgate_out[0, pl.ds(c * chunk, chunk), :] = both[:, :units]
            dup_out[0, pl.ds(c * chunk, chunk), :] = both[:, units:]

    def weight_grads_out():
        hidden = hidden_all[...].astype(F32).T.astype(BF16)
        for c in range(0, ring * ring, 2):
            pair = jnp.concatenate(
                [g_all[c // ring, c % ring], g_all[(c + 1) // ring, (c + 1) % ring]], axis=1
            )
            ddown_out[0, :, pl.ds(c * chunk, 2 * chunk)] = jnp.dot(
                hidden, pair, preferred_element_type=F32
            ).astype(BF16)

    count = len(BLOCKS)
    pick_g(0)
    pick_g(1)
    pick_x(0)
    pick_x(1)
    for block in range(2, count):
        pick_g(block)
        pick_x(block)
    for load in loads:
        load.wait()
    stages = ((relay, -2), (spread, -1), (forward, 0), (compute, 1), (fold, 2), (reduce_first, 3), (reduce_second, 4))
    for turn in range(-2, count + 3):
        if turn == count + 1:
            weight_grads_in()
        if turn == count + 2:
            weight_grads_out()
        for stage, lag in stages:
            block = turn - lag
            if stage in (reduce_first, reduce_second):
                if 0 <= block < last:
                    stage(block)
                if block + 1 == last:
                    stage(last)
            elif 0 <= block < count:
                stage(block)

    for copy in back_copies.values():
        copy.wait_recv()
    returned = back_recv[...].reshape(experts * wide, chunk)
    dinput_out[...] = lax.dot_general(
        token_hot[...], returned, (((0,), (0,)), ((), ())), preferred_element_type=F32
    ).astype(BF16)
    for copy in started:
        copy.wait_send()


def write_out(*refs):
    sources, targets, sem = refs[:4], refs[4:8], refs[8]
    copies = []
    for source, target in zip(sources, targets):
        if len(source.shape) == 2:
            copies.append((source, target))
        else:
            size = source.shape[1] // 4
            for part in range(4):
                piece = pl.ds(part * size, size)
                copies.append((source.at[:, piece], target.at[:, piece]))
    copies = [
        pltpu.make_async_copy(source, target, sem.at[number])
        for number, (source, target) in enumerate(copies)
    ]
    for copy in copies:
        copy.start()
    for copy in copies:
        copy.wait()


def local(
    grad_out,
    gate_prob,
    expert_ids,
    slot_index,
    saved_rows,
    row_rank,
    part_counts,
    w_gate,
    w_up,
    w_down,
):
    experts, cap = row_rank.shape[1], row_rank.shape[2]
    tokens, chunk = grad_out.shape
    ring = part_counts.shape[1]
    keep = saved_rows.shape[1]
    width, units = w_gate.shape[1], w_gate.shape[2]
    slots = experts * cap
    wide = 48
    copies = 2 * (experts - 1) + 3 + len(BLOCKS) * (8 + 8 + 12 + 6)
    vmem = pl.BlockSpec(memory_space=pltpu.VMEM)
    anywhere = pl.BlockSpec(memory_space=pl.ANY)
    held = pl.pallas_call(
        functools.partial(kernel, cap),
        out_shape=(
            pltpu.VMEM((tokens, chunk), BF16),
            pltpu.VMEM(w_gate.shape, BF16),
            pltpu.VMEM(w_up.shape, BF16),
            pltpu.VMEM(w_down.shape, BF16),
        ),
        in_specs=[anywhere] * 10,
        out_specs=(vmem,) * 4,
        scratch_shapes=[
            pltpu.VMEM((tokens, chunk), BF16),
            pltpu.VMEM((1, tokens), F32),
            pltpu.VMEM((1, tokens), jnp.int32),
            pltpu.VMEM((1, tokens), jnp.int32),
            pltpu.VMEM((experts, cap), jnp.int32),
            pltpu.VMEM((1, ring), jnp.int32),
            pltpu.VMEM((width, units), BF16),
            pltpu.VMEM((width, units), BF16),
            pltpu.VMEM((units, width), BF16),
            pltpu.VMEM((experts * wide, tokens), BF16),
            pltpu.VMEM((slots, ring * keep), BF16),
            pltpu.VMEM((experts, wide, chunk), BF16),
            pltpu.VMEM((experts, wide, chunk), BF16),
            pltpu.VMEM((ring, keep, chunk), BF16),
            pltpu.VMEM((ring, ring, slots, chunk), BF16),
            pltpu.VMEM((ring, ring, slots, chunk), BF16),
            pltpu.VMEM((slots, units), BF16),
            pltpu.VMEM((slots, 2 * units), BF16),
            pltpu.VMEM((ring, ring, slots, chunk), BF16),
            pltpu.VMEM((2, ring // 2, slots, chunk), BF16),
            pltpu.VMEM((ring - 1, ring, slots, chunk), BF16),
            pltpu.VMEM((ring, slots, chunk), BF16),
            pltpu.VMEM((ring - 1, slots, chunk), BF16),
            pltpu.VMEM((experts, wide, chunk), BF16),
            pltpu.VMEM((experts, wide, chunk), BF16),
            pltpu.SemaphoreType.DMA((10,)),
            pltpu.SemaphoreType.DMA((copies,)),
            pltpu.SemaphoreType.DMA((copies,)),
        ],
        compiler_params=pltpu.CompilerParams(
            collective_id=0, has_side_effects=True, vmem_limit_bytes=52 << 20
        ),
        name="experts_backward",
    )(
        grad_out,
        gate_prob.reshape(1, tokens),
        expert_ids.reshape(1, tokens),
        slot_index.reshape(1, tokens),
        saved_rows,
        row_rank,
        part_counts,
        w_gate,
        w_up,
        w_down,
    )
    held = [pltpu.with_memory_space_constraint(part, pltpu.VMEM) for part in held]
    return pl.pallas_call(
        write_out,
        out_shape=tuple(jax.ShapeDtypeStruct(part.shape, part.dtype) for part in held),
        in_specs=[vmem] * 4,
        out_specs=(anywhere,) * 4,
        scratch_shapes=[pltpu.SemaphoreType.DMA((13,))],
        name="write_out",
    )(*held)


def solution(mesh):
    placed = (
        P("expert", ("dp", "tensor")),
        P("expert"),
        P("expert"),
        P("expert"),
        P("expert", "dp", None),
        P("expert", None, None),
        P("expert", None),
        P("expert", None, ("dp", "tensor")),
        P("expert", None, ("dp", "tensor")),
        P("expert", ("dp", "tensor"), None),
    )
    return jax.shard_map(
        local,
        mesh=mesh,
        in_specs=placed,
        out_specs=(
            P("expert", ("dp", "tensor")),
            P("expert", None, ("dp", "tensor")),
            P("expert", None, ("dp", "tensor")),
            P("expert", ("dp", "tensor"), None),
        ),
        check_vma=False,
    )
```

time: 83.3 us -> 75.4 us (0.905)
  local copies, waits for them, and re-layouts: 6.49 us -> 0 us
  Pallas kernels: 75.9 us -> 74.7 us
    unnamed x8 -> x0, local copies, waits for them, and re-layouts: 6.49 us -> none
    pallas_call x1 -> x2, Pallas kernels: 75.9 us -> 74.7 us  [the longest x1 72.8 us: local(): pl.pallas_call(functools.partial(kernel, cap), out_shape=(pltpu.VMEM((tok...]
where the time goes in v2:
time: 75.4 us; the launch traced here: 75.3 us
  Pallas kernels  74.7 us (99%)
    pallas_call x1, Pallas kernels, local(): pl.pallas_call(functools.partial(kernel, cap), out_shape=(pltpu.VMEM((tok...  72.8 us
    pallas_call x1, Pallas kernels, local(): pl.pallas_call(write_out, out_shape=tuple((jax.ShapeDtypeStruct(part.shap...  1.81 us

profile of v2, /device:TPU:1, one launch (start us, length us, event | category | flops | bytes accessed | tf_op | source)
XLA Modules:
  0.0 75.3 jit_solution(7228631860912683652)
XLA Ops:
  0.6 72.8 %experts_backward.1 = (bf16[512,128]{1,0:T(8,128)(2,1)S(1)}, bf16[1,2048,256]{2,1,0:T(8,128)(2,1)S(1)}, bf16[1,2048,256]{2,1,0:T(8,128)(2,1)S(1)}, bf16[1,256,2048]{2,1,0:T(8,128)(2,1)S(1)}) custom-call(bf16[512,128]{1,0:T(8,128)(2,1)} %grad_hbm.1, f32[1,512]{1,0:T(1,128)} %bitcast.3, s32[1,512]{1,0:T(1,128)} %bitcast.4, s32[1,512]{1,0:T(1,128)} %bitcast.5, ...), custom_call_target="tpu_custom_call" | custom-call | tf_op jit(solution)/shard_map/experts_backward/pallas_call | solution.py:499
  73.5 1.8 %write_out.1 = (bf16[512,128]{1,0:T(8,128)(2,1)}, bf16[1,2048,256]{2,1,0:T(8,128)(2,1)}, bf16[1,2048,256]{2,1,0:T(8,128)(2,1)}, bf16[1,256,2048]{2,1,0:T(8,128)(2,1)}) custom-call(bf16[512,128]{1,0:T(8,128)(2,1)S(1)} %get-tuple-element.8.refs_0_, bf16[1,2048,256]{2,1,0:T(8,128)(2,1)S(1)} %get-tuple-element.9.refs_1_, ...), custom_call_target="tpu_custom_call" | custom-call | tf_op jit(solution)/shard_map/write_out/pallas_call | solution.py:556

commit v3 on v2

--- a/solution.py
+++ b/solution.py
@@ -12,6 +12,7 @@
 BLOCKS = (4, 4, 4, 4)
 DIRECT_SHARES = 1
 DIRECT_SUMS = 1
+SPLIT = 2.5
 OFFSETS = (-2, 3, -3, 4, -4, 5, -5, 6, -6, 7, -7, 8, 0, 1, -1, 2)
 
 
@@ -41,6 +42,9 @@
     w_up,
     w_down,
     token_hot,
+    token_hot_t,
+    w_down_t,
+    w_both_t,
     row_hot,
     bin_send,
     bin_recv,
@@ -76,9 +80,9 @@
     def span_of(block):
         return pl.ds(*rows_of(block))
 
-    def halves_of(block):
+    def halves_of(block, share=2.5):
         start, size = rows_of(block)
-        cut = size // 32 * 16
+        cut = int(size * share / 5) // 16 * 16
         return (pl.ds(start, cut), pl.ds(start + cut, size - cut))
 
     started = []
@@ -189,21 +193,36 @@
             parts.append(jnp.where(column == position, 1.0, 0.0))
         row_hot[span_of(block), :] = jnp.concatenate(parts, axis=0).astype(BF16)
 
+    token_hot_t[...] = token_hot[...].astype(F32).T.astype(BF16)
+    for load in loads:
+        load.wait()
+    w_down_t[...] = w_down[...].astype(F32).T.astype(BF16)
+    w_both_t[pl.ds(0, units), :] = w_gate[...].astype(F32).T.astype(BF16)
+    w_both_t[pl.ds(units, units), :] = w_up[...].astype(F32).T.astype(BF16)
+
     x_first, g_first = {}, {}
 
-    def share(block, ref, device):
-        piece = ref.at[mx, my, span_of(block)]
-        return [remote(piece, piece, device(step)) for step in ((2, 1, 3) if block < DIRECT_SHARES else (1, 3))]
+    def share_x(block):
+        span = span_of(block)
+        piece = x_all.at[0, my, span]
+        steps = (2, 1, 3) if block < DIRECT_SHARES else (1, 3)
+        return [remote(piece, x_all.at[ring - step, my, span], xdev(step)) for step in steps]
+
+    def share_g(block):
+        span = span_of(block)
+        piece = g_all.at[mx, 0, span]
+        steps = (2, 1, 3) if block < DIRECT_SHARES else (1, 3)
+        return [remote(piece, g_all.at[mx, ring - step, span], ydev(step)) for step in steps]
 
     def pick_x(block):
         if block == 0:
             for copy in saved_copies:
                 copy.wait_recv()
         span = span_of(block)
-        x_all[mx, my, span, :] = jnp.dot(
+        x_all[0, my, span, :] = jnp.dot(
             row_hot[span, :], saved_recv[...].reshape(ring * keep, chunk), preferred_element_type=F32
         ).astype(BF16)
-        x_first[block] = share(block, x_all, xdev)
+        x_first[block] = share_x(block)
 
     def pick_g(block):
         parts = []
@@ -214,8 +233,8 @@
                 bin_copies[spot].wait_recv()
                 piece = bin_recv[spot]
             parts.append(piece.astype(F32)[:cap])
-        g_all[mx, my, span_of(block), :] = jnp.concatenate(parts, axis=0).astype(BF16)
-        g_first[block] = share(block, g_all, ydev)
+        g_all[mx, 0, span_of(block), :] = jnp.concatenate(parts, axis=0).astype(BF16)
+        g_first[block] = share_g(block)
 
     low_x, high_x = lax.rem(mx + ring - 1, ring), lax.rem(mx + 1, ring)
     low_y, high_y = lax.rem(my + ring - 1, ring), lax.rem(my + 1, ring)
@@ -224,30 +243,60 @@
         if block < DIRECT_SHARES:
             return
         first, second = halves_of(block)
-        for copies, ref, low, high, device in (
-            (x_first, x_all, (low_x, my), (high_x, my), xdev),
-            (g_first, g_all, (mx, low_y), (mx, high_y), ydev),
+        up, down = x_first[block]
+        up.wait_recv()
+        sent = [remote(x_all.at[ring - 1, my, first], x_all.at[ring - 2, my, first], xdev(1))]
+        down.wait_recv()
+        sent.append(remote(x_all.at[1, my, second], x_all.at[2, my, second], xdev(-1)))
+        x_first[block] = sent
+        up, down = g_first[block]
+        up.wait_recv()
+        sent = [remote(g_all.at[mx, ring - 1, first], g_all.at[mx, ring - 2, first], ydev(1))]
+        down.wait_recv()
+        sent.append(remote(g_all.at[mx, 1, second], g_all.at[mx, 2, second], ydev(-1)))
+        g_first[block] = sent
+
+    x_own, g_own = [], []
+
+    def two_blocks(part):
+        return first_group[2 * part] * cap, sum(BLOCKS[2 * part : 2 * part + 2]) * cap
+
+    def send_own(part, own, piece, cross):
+        own.append([remote(piece, piece, cross(1)), remote(piece, piece, cross(-1))])
+
+    def send_own_x(part):
+        send_own(part, x_own, x_all.at[0, my, pl.ds(*two_blocks(part))], ydev)
+
+    def send_own_g(part):
+        send_own(part, g_own, g_all.at[mx, 0, pl.ds(*two_blocks(part))], xdev)
+
+    def forward_own(part):
+        start, size = two_blocks(part)
+        cut = size // 32 * 16
+        first, second = pl.ds(start, cut), pl.ds(start + cut, size - cut)
+        for own, low, high, cross in (
+            (x_own, x_all.at[0, low_y, first], x_all.at[0, high_y, second], ydev),
+            (g_own, g_all.at[low_x, 0, first], g_all.at[high_x, 0, second], xdev),
         ):
-            up, down = copies[block]
+            up, down = own[part]
             up.wait_recv()
-            piece = ref.at[low[0], low[1], first]
-            sent = [remote(piece, piece, device(1))]
+            sent = [remote(low, low, cross(1))]
             down.wait_recv()
-            piece = ref.at[high[0], high[1], second]
-            sent.append(remote(piece, piece, device(-1)))
-            copies[block] = sent
+            sent.append(remote(high, high, cross(-1)))
+            own[part] = sent
 
     near, far = {}, {}
+    others = pl.ds(1, ring - 1)
 
     def spread(block):
         span = span_of(block)
         for copy in x_first[block]:
             copy.wait_recv()
-        piece = x_all.at[:, my, span]
+        piece = x_all.at[others, my, span]
         x_near = [remote(piece, piece, ydev(1)), remote(piece, piece, ydev(-1))]
         for copy in g_first[block]:
             copy.wait_recv()
-        piece = g_all.at[mx, :, span]
+        piece = g_all.at[mx, others, span]
         g_near = [remote(piece, piece, xdev(1)), remote(piece, piece, xdev(-1))]
         near[block] = (x_near, g_near)
 
@@ -256,17 +305,18 @@
     def forward(block):
         span = span_of(block)
         x_near, g_near = near[block]
+        first, second = (pl.ds(1, 1), pl.ds(2, 2)) if block % 2 else (pl.ds(1, 2), pl.ds(3, 1))
         x_near[0].wait_recv()
-        piece = x_all.at[low_half, low_y, span]
+        piece = x_all.at[first, low_y, span]
         copies = [remote(piece, piece, ydev(1))]
         x_near[1].wait_recv()
-        piece = x_all.at[high_half, high_y, span]
+        piece = x_all.at[second, high_y, span]
         copies.append(remote(piece, piece, ydev(-1)))
         g_near[0].wait_recv()
-        piece = g_all.at[low_x, low_half, span]
+        piece = g_all.at[low_x, first, span]
         copies.append(remote(piece, piece, xdev(1)))
         g_near[1].wait_recv()
-        piece = g_all.at[high_x, high_half, span]
+        piece = g_all.at[high_x, second, span]
         copies.append(remote(piece, piece, xdev(-1)))
         far[block] = copies
 
@@ -279,21 +329,28 @@
     )
     part_copies, half_copies, back_copies = {}, {}, {}
 
+    def y_place(c):
+        return lax.rem(c % ring + ring - my, ring)
+
+    def x_place(c):
+        return lax.rem(c // ring + ring - mx, ring)
+
     def compute(block):
         span = span_of(block)
+        if block % 2 == 0:
+            for copy in x_own[block // 2] + g_own[block // 2]:
+                copy.wait_recv()
         for copy in far[block]:
             copy.wait_recv()
         inputs = jnp.concatenate(
-            [x_all[c // ring, c % ring, span, :] for c in range(ring * ring)], axis=1
+            [x_all[x_place(c), c % ring, span, :] for c in range(ring * ring)], axis=1
         )
         gate_pre = jnp.dot(inputs, w_gate[...], preferred_element_type=F32)
         up_pre = jnp.dot(inputs, w_up[...], preferred_element_type=F32)
         grads = jnp.concatenate(
-            [g_all[c // ring, c % ring, span, :] for c in range(ring * ring)], axis=1
+            [g_all[c // ring, y_place(c), span, :] for c in range(ring * ring)], axis=1
         )
-        hidden_grad = lax.dot_general(
-            grads, w_down[...], (((1,), (1,)), ((), ())), preferred_element_type=F32
-        )
+        hidden_grad = jnp.dot(grads, w_down_t[...], preferred_element_type=F32)
         squash = 1.0 / (1.0 + jnp.exp(-gate_pre))
         activated = gate_pre * squash
         hidden_all[span, :] = (activated * up_pre).astype(BF16)
@@ -301,18 +358,15 @@
         gate_grad = (hidden_grad * up_pre * squash * (1.0 + gate_pre * (1.0 - squash))).astype(BF16)
         both_all[span, pl.ds(0, units)] = gate_grad
         both_all[span, pl.ds(units, units)] = up_grad
+        both = jnp.concatenate([gate_grad, up_grad], axis=1)
         for x in range(ring):
             piece = pl.ds(x * ring * chunk, ring * chunk)
-            total = lax.dot_general(
-                gate_grad, w_gate[piece, :], (((1,), (1,)), ((), ())), preferred_element_type=F32
-            ) + lax.dot_general(
-                up_grad, w_up[piece, :], (((1,), (1,)), ((), ())), preferred_element_type=F32
-            )
+            total = jnp.dot(both, w_both_t[:, piece], preferred_element_type=F32)
             total = total.astype(BF16)
             for y in range(ring):
                 part_send[x, y, span, :] = total[:, y * chunk : (y + 1) * chunk]
         copies = [[], []]
-        for which, span in enumerate(halves_of(block)):
+        for which, span in enumerate(halves_of(block, SPLIT)):
             device, mine, low, high = lines[which][:4]
             if block > last - DIRECT_SUMS:
                 for step in (2, 1, 3):
@@ -341,7 +395,7 @@
     def fold(block):
         if block > last - DIRECT_SUMS:
             return
-        for which, span in enumerate(halves_of(block)):
+        for which, span in enumerate(halves_of(block, SPLIT)):
             device, mine, low, high = lines[which][:4]
             copies = part_copies[block][which]
             for number, (index, others, step) in enumerate(
@@ -357,7 +411,7 @@
 
     def reduce_first(block):
         sent = [[], []]
-        for which, span in enumerate(halves_of(block)):
+        for which, span in enumerate(halves_of(block, SPLIT)):
             mine = lines[which][1]
             device, own = lines[which][4:]
             for copy in part_copies[block][which]:
@@ -376,7 +430,7 @@
     def reduce_second(block):
         spare = jnp.zeros((wide - cap, chunk), F32)
         totals = []
-        for which, span in enumerate(halves_of(block)):
+        for which, span in enumerate(halves_of(block, SPLIT)):
             own = lines[which][5]
             for copy in half_copies[block][which]:
                 copy.wait_recv()
@@ -399,7 +453,7 @@
     def weight_grads_in():
         for c in range(ring * ring):
             both = lax.dot_general(
-                x_all[c // ring, c % ring],
+                x_all[x_place(c), c % ring],
                 both_all[...],
                 (((0,), (0,)), ((), ())),
                 preferred_element_type=F32,
@@ -411,7 +465,7 @@
         hidden = hidden_all[...].astype(F32).T.astype(BF16)
         for c in range(0, ring * ring, 2):
             pair = jnp.concatenate(
-                [g_all[c // ring, c % ring], g_all[(c + 1) // ring, (c + 1) % ring]], axis=1
+                [g_all[c // ring, y_place(c)], g_all[c // ring, y_place(c + 1)]], axis=1
             )
             ddown_out[0, :, pl.ds(c * chunk, 2 * chunk)] = jnp.dot(
                 hidden, pair, preferred_element_type=F32
@@ -420,19 +474,24 @@
     count = len(BLOCKS)
     pick_g(0)
     pick_g(1)
+    send_own_g(0)
     pick_x(0)
     pick_x(1)
-    for block in range(2, count):
-        pick_g(block)
-        pick_x(block)
-    for load in loads:
-        load.wait()
+    send_own_x(0)
+    pick_g(2)
+    pick_x(2)
+    pick_g(3)
+    pick_x(3)
+    send_own_x(1)
+    send_own_g(1)
     stages = ((relay, -2), (spread, -1), (forward, 0), (compute, 1), (fold, 2), (reduce_first, 3), (reduce_second, 4))
     for turn in range(-2, count + 3):
         if turn == count + 1:
             weight_grads_in()
         if turn == count + 2:
             weight_grads_out()
+        if turn in (-1, 0):
+            forward_own(turn + 1)
         for stage, lag in stages:
             block = turn - lag
             if stage in (reduce_first, reduce_second):
@@ -446,9 +505,7 @@
     for copy in back_copies.values():
         copy.wait_recv()
     returned = back_recv[...].reshape(experts * wide, chunk)
-    dinput_out[...] = lax.dot_general(
-        token_hot[...], returned, (((0,), (0,)), ((), ())), preferred_element_type=F32
-    ).astype(BF16)
+    dinput_out[...] = jnp.dot(token_hot_t[...], returned, preferred_element_type=F32).astype(BF16)
     for copy in started:
         copy.wait_send()
 
@@ -493,7 +550,7 @@
     width, units = w_gate.shape[1], w_gate.shape[2]
     slots = experts * cap
     wide = 48
-    copies = 2 * (experts - 1) + 3 + len(BLOCKS) * (8 + 8 + 12 + 6)
+    copies = 2 * (experts - 1) + 3 + len(BLOCKS) * (8 + 8 + 12 + 6) + 16
     vmem = pl.BlockSpec(memory_space=pltpu.VMEM)
     anywhere = pl.BlockSpec(memory_space=pl.ANY)
     held = pl.pallas_call(
@@ -517,6 +574,9 @@
             pltpu.VMEM((width, units), BF16),
             pltpu.VMEM((units, width), BF16),
             pltpu.VMEM((experts * wide, tokens), BF16),
+            pltpu.VMEM((tokens, experts * wide), BF16),
+            pltpu.VMEM((width, units), BF16),
+            pltpu.VMEM((2 * units, width), BF16),
             pltpu.VMEM((slots, ring * keep), BF16),
             pltpu.VMEM((experts, wide, chunk), BF16),
             pltpu.VMEM((experts, wide, chunk), BF16),

time: 75.4 us -> 74 us (0.981)
  Pallas kernels: 74.7 us -> 73.3 us
    pallas_call x1, Pallas kernels: 72.8 us -> 71.5 us  [local(): pl.pallas_call(functools.partial(kernel, cap), out_shape=(pltpu.VMEM((tok...]
where the time goes in v3:
time: 74 us; the launch traced here: 73.9 us
  Pallas kernels  73.3 us (99%)
    pallas_call x1, Pallas kernels, local(): pl.pallas_call(functools.partial(kernel, cap), out_shape=(pltpu.VMEM((tok...  71.5 us
    pallas_call x1, Pallas kernels, local(): pl.pallas_call(write_out, out_shape=tuple((jax.ShapeDtypeStruct(part.shap...  1.81 us

profile of v3, /device:TPU:1, one launch (start us, length us, event | category | flops | bytes accessed | tf_op | source)
XLA Modules:
  0.0 73.9 jit_solution(3507792567471430386)
XLA Ops:
  0.6 71.5 %experts_backward.1 = (bf16[512,128]{1,0:T(8,128)(2,1)S(1)}, bf16[1,2048,256]{2,1,0:T(8,128)(2,1)S(1)}, bf16[1,2048,256]{2,1,0:T(8,128)(2,1)S(1)}, bf16[1,256,2048]{2,1,0:T(8,128)(2,1)S(1)}) custom-call(bf16[512,128]{1,0:T(8,128)(2,1)} %grad_hbm.1, f32[1,512]{1,0:T(1,128)} %bitcast.3, s32[1,512]{1,0:T(1,128)} %bitcast.4, s32[1,512]{1,0:T(1,128)} %bitcast.5, ...), custom_call_target="tpu_custom_call" | custom-call | tf_op jit(solution)/shard_map/experts_backward/pallas_call | solution.py:556
  72.1 1.8 %write_out.1 = (bf16[512,128]{1,0:T(8,128)(2,1)}, bf16[1,2048,256]{2,1,0:T(8,128)(2,1)}, bf16[1,2048,256]{2,1,0:T(8,128)(2,1)}, bf16[1,256,2048]{2,1,0:T(8,128)(2,1)}) custom-call(bf16[512,128]{1,0:T(8,128)(2,1)S(1)} %get-tuple-element.8.refs_0_, bf16[1,2048,256]{2,1,0:T(8,128)(2,1)S(1)} %get-tuple-element.9.refs_1_, ...), custom_call_target="tpu_custom_call" | custom-call | tf_op jit(solution)/shard_map/write_out/pallas_call | solution.py:616

commit v4 on v3

--- a/solution.py
+++ b/solution.py
@@ -485,22 +485,23 @@
     send_own_x(1)
     send_own_g(1)
     stages = ((relay, -2), (spread, -1), (forward, 0), (compute, 1), (fold, 2), (reduce_first, 3), (reduce_second, 4))
-    for turn in range(-2, count + 3):
-        if turn == count + 1:
-            weight_grads_in()
-        if turn == count + 2:
-            weight_grads_out()
+    for turn in range(-2, count):
         if turn in (-1, 0):
             forward_own(turn + 1)
         for stage, lag in stages:
-            block = turn - lag
-            if stage in (reduce_first, reduce_second):
-                if 0 <= block < last:
-                    stage(block)
-                if block + 1 == last:
-                    stage(last)
-            elif 0 <= block < count:
-                stage(block)
+            if 0 <= turn - lag < count:
+                stage(turn - lag)
+    compute(last)
+    fold(last - 1)
+    reduce_first(last - 2)
+    reduce_second(last - 3)
+    weight_grads_in()
+    reduce_first(last - 1)
+    reduce_second(last - 2)
+    reduce_first(last)
+    reduce_second(last - 1)
+    weight_grads_out()
+    reduce_second(last)
 
     for copy in back_copies.values():
         copy.wait_recv()

time: 74 us -> 74 us (level)
  no operation moved by 1% of the time
where the time goes in v4:
time: 74 us; the launch traced here: 73.9 us
  Pallas kernels  73.3 us (99%)
    pallas_call x1, Pallas kernels, local(): pl.pallas_call(functools.partial(kernel, cap), out_shape=(pltpu.VMEM((tok...  71.5 us
    pallas_call x1, Pallas kernels, local(): pl.pallas_call(write_out, out_shape=tuple((jax.ShapeDtypeStruct(part.shap...  1.81 us

profile of v4, /device:TPU:1, one launch (start us, length us, event | category | flops | bytes accessed | tf_op | source)
XLA Modules:
  0.0 73.9 jit_solution(15932533566720773851)
XLA Ops:
  0.6 71.5 %experts_backward.1 = (bf16[512,128]{1,0:T(8,128)(2,1)S(1)}, bf16[1,2048,256]{2,1,0:T(8,128)(2,1)S(1)}, bf16[1,2048,256]{2,1,0:T(8,128)(2,1)S(1)}, bf16[1,256,2048]{2,1,0:T(8,128)(2,1)S(1)}) custom-call(bf16[512,128]{1,0:T(8,128)(2,1)} %grad_hbm.1, f32[1,512]{1,0:T(1,128)} %bitcast.3, s32[1,512]{1,0:T(1,128)} %bitcast.4, s32[1,512]{1,0:T(1,128)} %bitcast.5, ...), custom_call_target="tpu_custom_call" | custom-call | tf_op jit(solution)/shard_map/experts_backward/pallas_call | solution.py:557
  72.1 1.8 %write_out.1 = (bf16[512,128]{1,0:T(8,128)(2,1)}, bf16[1,2048,256]{2,1,0:T(8,128)(2,1)}, bf16[1,2048,256]{2,1,0:T(8,128)(2,1)}, bf16[1,256,2048]{2,1,0:T(8,128)(2,1)}) custom-call(bf16[512,128]{1,0:T(8,128)(2,1)S(1)} %get-tuple-element.8.refs_0_, bf16[1,2048,256]{2,1,0:T(8,128)(2,1)S(1)} %get-tuple-element.9.refs_1_, ...), custom_call_target="tpu_custom_call" | custom-call | tf_op jit(solution)/shard_map/write_out/pallas_call | solution.py:617
